TPU v7x, 512 devices: a whole 4x8x8 slice. The times are simulated.
512 devices in a mesh: dp: 2 (over core), ctx: 32 (over z_hi, y), tp: 8 (over z_lo, x).
Axes of the slice: x: 4, y: 8, z: 8 (z_hi: 4, z_lo: 2; z = z_hi * 2 + z_lo), core: 2. Of those that a mesh axis runs over, the one named last changes fastest.
Arguments:
- q_in: bfloat16 [2, 4096, 5120], P('dp', 'ctx', 'tp'), may hold values from -10 to 10
- key_input: bfloat16 [2, 4096, 1024], P('dp', 'ctx', 'tp'), may hold values from -10 to 10
- value_input: bfloat16 [2, 4096, 1024], P('dp', 'ctx', 'tp'), may hold values from -6 to 6
- q_bias: float32 [5120], P('tp'), may hold values from -3 to 3
- key_bias: float32 [1024], P('tp'), may hold values from -3 to 3
- value_bias: float32 [1024], P('tp'), may hold values from -3 to 3
- out_weight: bfloat16 [5120, 5120], P('tp', 'dp'), may hold values from -0.078125 to 0.078125
- out_grad: bfloat16 [2, 4096, 5120], P('dp', ('ctx', 'tp')), may hold values from -5 to 5
- doc_lengths: int32 [2, 8], P('dp'), may hold values from 1 to 2048, 4096 in all within a row
- block_pos: int32 [2, 32, 2], P('dp'), may hold values from 0 to 63, as said below
Outputs:
- out: bfloat16 [2, 4096, 5120], P('dp', ('ctx', 'tp'))
- q_grad: bfloat16 [2, 4096, 5120], P('dp', 'ctx', 'tp')
- k_grad: bfloat16 [2, 4096, 1024], P('dp', 'ctx', 'tp')
- v_grad: bfloat16 [2, 4096, 1024], P('dp', 'ctx', 'tp')
- q_bias_grad: float32 [5120], P('tp')
- k_bias_grad: float32 [1024], P('tp')
- v_bias_grad: float32 [1024], P('tp')
Inputs may be any that keep to these rules, and one draw needn't show every extreme that they name: `block_pos`: for each sequence, the first entries over the indices of ctx are a permutation of 0 to 31, and each second entry is 63 minus the first entry beside it.
All inputs are finite; a program needn't handle non-finite values.
Results may differ from a plain program's by a relative error of at most 0.04.
Values may be sent and summed in bfloat16 or wider, within the bound.
A program may use at most 64 MiB of HBM per device.

v0:
```python
import jax
import jax.numpy as jnp
from jax import lax
from jax.sharding import PartitionSpec as P

HEAD_WIDTH = 128


ROPE_BASE = 1000000.0


def positions(blocks, block_width):
    offsets = jnp.arange(block_width, dtype=jnp.int32)
    starts = blocks[:, :, None] * block_width
    return (starts + offsets[None, None, :]).reshape(-1)


def documents(lengths, token_pos):
    doc_ends = jnp.cumsum(lengths)
    return jnp.sum((doc_ends[None, :] <= token_pos[:, None]).astype(jnp.int32), axis=1)


def rotary(token_pos, head_size):
    frequency = ROPE_BASE ** (-jnp.arange(0, head_size, 2).astype(jnp.float32) / head_size)
    phases = token_pos.astype(jnp.float32)[:, None] * frequency[None, :]
    phases = jnp.concatenate([phases, phases], axis=1)
    return (jnp.cos(phases)[:, None, :], jnp.sin(phases)[:, None, :])


def apply_rotary(field, cosine_values, sine_values):
    half_width = field.shape[-1] // 2
    turned = jnp.concatenate([-field[..., half_width:], field[..., :half_width]], axis=-1)
    return field * cosine_values + turned * sine_values


def shards(
    q_in,
    key_input,
    value_input,
    q_bias,
    key_bias,
    value_bias,
    out_weight,
    out_grad,
    doc_lengths,
    block_pos,
):
    score_scale = HEAD_WIDTH ** (-0.5)
    row_count = q_in.shape[1]
    q_width = q_in.shape[2]
    k_width = key_input.shape[2]
    q_heads = q_width // HEAD_WIDTH
    k_heads = k_width // HEAD_WIDTH
    group_size = q_heads // k_heads
    ctx_index = lax.axis_index("ctx")
    token_pos = positions(block_pos[0], row_count // 2)
    token_doc = documents(doc_lengths[0], token_pos)
    own_pos = lax.dynamic_slice_in_dim(token_pos, ctx_index * row_count, row_count)
    own_doc = lax.dynamic_slice_in_dim(token_doc, ctx_index * row_count, row_count)
    cosine_values, sine_values = rotary(own_pos, HEAD_WIDTH)
    query = apply_rotary(
        q_in[0].astype(jnp.float32).reshape(row_count, q_heads, HEAD_WIDTH)
        + q_bias.reshape(q_heads, HEAD_WIDTH),
        cosine_values,
        sine_values,
    ).astype(jnp.bfloat16)
    key_row_block = apply_rotary(
        key_input[0].astype(jnp.float32).reshape(row_count, k_heads, HEAD_WIDTH)
        + key_bias.reshape(k_heads, HEAD_WIDTH),
        cosine_values,
        sine_values,
    ).astype(jnp.bfloat16)
    value_row_block = (value_input[0].astype(jnp.float32) + value_bias).astype(jnp.bfloat16)
    key_all, value_all = (
        lax.all_gather(key_row_block.reshape(row_count, k_width), "ctx", axis=0, tiled=True),
        lax.all_gather(value_row_block, "ctx", axis=0, tiled=True),
    )
    key_all = key_all.reshape(-1, k_heads, HEAD_WIDTH)
    value_all = value_all.reshape(-1, k_heads, HEAD_WIDTH)
    grouped_heads = query.reshape(row_count, k_heads, group_size, HEAD_WIDTH)
    scores = (
        jnp.einsum("rkgd,lkd->kgrl", grouped_heads, key_all, preferred_element_type=jnp.float32)
        * score_scale
    )
    allowed = (token_pos[None, :] <= own_pos[:, None]) & (token_doc[None, :] == own_doc[:, None])
    scores = jnp.where(allowed[None, None], scores, -jnp.inf)
    row_max = jnp.max(scores, axis=3, keepdims=True)
    row_sum = jnp.sum(jnp.exp(scores - row_max), axis=3, keepdims=True)
    probability = jnp.exp(scores - (row_max + jnp.log(row_sum))).astype(jnp.bfloat16)
    attended_output = (
        jnp.einsum("kgrl,lkd->rkgd", probability, value_all, preferred_element_type=jnp.float32)
        .astype(jnp.bfloat16)
        .reshape(row_count, q_width)
    )
    contract_last = (((1,), (1,)), ((), ()))
    full_weight = lax.all_gather(out_weight, "dp", axis=1, tiled=True)
    mixed_rows = lax.psum_scatter(
        jnp.dot(attended_output, full_weight, preferred_element_type=jnp.float32).astype(
            jnp.bfloat16
        ),
        "tp",
        scatter_dimension=0,
        tiled=True,
    )
    attended_gradient = lax.dot_general(
        lax.all_gather(out_grad[0], "tp", axis=0, tiled=True),
        full_weight,
        contract_last,
        preferred_element_type=jnp.float32,
    )
    attended_gradient = attended_gradient.astype(jnp.bfloat16)
    grad_grouped = attended_gradient.reshape(row_count, k_heads, group_size, HEAD_WIDTH)
    grad_prob = jnp.einsum(
        "rkgd,lkd->kgrl", grad_grouped, value_all, preferred_element_type=jnp.float32
    )
    row_correction = jnp.sum(
        grad_grouped.astype(jnp.float32)
        * attended_output.reshape(row_count, k_heads, group_size, HEAD_WIDTH).astype(jnp.float32),
        axis=3,
    )
    row_correction = jnp.transpose(row_correction, (1, 2, 0))[..., None]
    grad_score = (probability.astype(jnp.float32) * (grad_prob - row_correction)).astype(
        jnp.bfloat16
    )
    grad_query = (
        jnp.einsum("kgrl,lkd->rkgd", grad_score, key_all, preferred_element_type=jnp.float32)
        * score_scale
    )
    key_part = (
        jnp.einsum("kgrl,rkgd->lkd", grad_score, grouped_heads, preferred_element_type=jnp.float32)
        * score_scale
    )
    value_part = jnp.einsum(
        "kgrl,rkgd->lkd", probability, grad_grouped, preferred_element_type=jnp.float32
    )
    kv_grads = lax.psum_scatter(
        jnp.concatenate(
            [
                key_part.reshape(row_count * lax.axis_size("ctx"), k_width),
                value_part.reshape(row_count * lax.axis_size("ctx"), k_width),
            ],
            axis=1,
        ).astype(jnp.bfloat16),
        "ctx",
        scatter_dimension=0,
        tiled=True,
    ).astype(jnp.float32)
    pre_query = apply_rotary(
        grad_query.reshape(row_count, q_heads, HEAD_WIDTH), cosine_values, -sine_values
    ).reshape(row_count, q_width)
    pre_key = apply_rotary(
        kv_grads[:, :k_width].reshape(row_count, k_heads, HEAD_WIDTH), cosine_values, -sine_values
    ).reshape(row_count, k_width)
    grad_value = kv_grads[:, k_width:]
    query_bias_sum, key_bias_sum, value_bias_sum = lax.psum(
        (jnp.sum(pre_query, axis=0), jnp.sum(pre_key, axis=0), jnp.sum(grad_value, axis=0)),
        ("dp", "ctx"),
    )
    return (
        mixed_rows[None],
        pre_query.astype(jnp.bfloat16)[None],
        pre_key.astype(jnp.bfloat16)[None],
        grad_value.astype(jnp.bfloat16)[None],
        query_bias_sum,
        key_bias_sum,
        value_bias_sum,
    )


def solution(mesh):
    return jax.shard_map(
        shards,
        mesh=mesh,
        in_specs=(
            P("dp", "ctx", "tp"),
            P("dp", "ctx", "tp"),
            P("dp", "ctx", "tp"),
            P("tp"),
            P("tp"),
            P("tp"),
            P("tp", "dp"),
            P("dp", ("ctx", "tp"), None),
            P("dp", None),
            P("dp", None, None),
        ),
        out_specs=(
            P("dp", ("ctx", "tp"), None),
            P("dp", "ctx", "tp"),
            P("dp", "ctx", "tp"),
            P("dp", "ctx", "tp"),
            P("tp"),
            P("tp"),
            P("tp"),
        ),
        check_vma=False,
    )
```

profile of v0, /device:TPU:6, one launch (start us, length us, event | category | flops | bytes accessed | tf_op | source)
XLA Modules:
  0.0 647.3 jit_solution(17493290743997894973)
XLA Ops:
  7.3 0.7 multiply_bitcast_fusion
  7.9 0.1 copy.63
  8.0 0.1 iota_add_fusion
  8.1 0.1 add.133
  8.2 0.8 fusion.44
  9.1 0.1 fusion.57
  9.2 0.1 broadcast_multiply_fusion.2
  9.2 1.8 broadcast_multiply_fusion.1
  11.1 0.7 all-gather.12.cloned.1.call-update
  11.8 0.7 all-gather.10.cloned.1.call-update
  12.6 0.9 copy.62
  13.4 1.4 fusion.48
  14.9 0.1 copy.66
  15.0 1.1 copy.64
  16.1 0.8 broadcast_add_fusion
  16.9 0.1 copy.65
  17.0 0.2 reduce-window.8
  17.2 0.1 convert_reduce_fusion
  17.3 0.1 dynamic_slice.7
  17.5 0.8 fusion.34
  18.3 1.4 compare_and_fusion
  19.7 80.7 %all-gather.8.cloned.1.call-done = bf16[4096,128]{1,0:T(8,128)(2,1)} async-done(((bf16[128,128]{1,0:T(8,128)(2,1)}), bf16[4096,128]{1,0:T(8,128)(2,1)}) %all-gather.8.cloned.1.call-update) | async-done | bytes 1048592 | tf_op jit(solution)/shard_map/all_gather | solution.py:75
  100.4 2.8 fusion.2
  103.2 2.2 exponential_reduce_fusion
  105.4 4.6 exponential_convert_fusion
  110.0 31.9 %all-gather.12.cloned.1.call-done = bf16[1,128,5120]{2,1,0:T(8,128)(2,1)} async-done(((bf16[1,16,5120]{2,1,0:T(8,128)(2,1)}), bf16[1,128,5120]{2,1,0:T(8,128)(2,1)}) %all-gather.12.cloned.1.call-update) | async-done | bytes 1310736 | tf_op jit(solution)/shard_map/all_gather | solution.py:106
  141.9 29.0 %all-gather.10.cloned.1.call-done = bf16[640,5120]{1,0:T(8,128)(2,1)} async-done(((bf16[640,2560]{1,0:T(8,128)(2,1)}), bf16[640,5120]{1,0:T(8,128)(2,1)}) %all-gather.10.cloned.1.call-update) | async-done | bytes 6553616 | tf_op jit(solution)/shard_map/all_gather | solution.py:96
  170.9 5.4 fusion.22
  176.3 0.1 copy.72
  176.5 0.2 copy.69
  176.7 4.0 fusion.16
  180.7 76.6 %all-gather.6.cloned.1.call-done = bf16[4096,128]{0,1:T(8,128)(2,1)} async-done(((bf16[128,128]{0,1:T(8,128)(2,1)}), bf16[4096,128]{0,1:T(8,128)(2,1)}) %all-gather.6.cloned.1.call-update) | async-done | bytes 1048592 | tf_op jit(solution)/shard_map/all_gather | solution.py:76
  257.3 3.9 multiply_reduce_fusion
  261.2 4.2 fusion.3
  265.4 2.4 copy-done
  267.8 1.8 fusion.19
  269.6 1.7 pad_maximum_fusion
  271.4 5.3 convolution_convert_fusion
  276.6 0.1 copy.75
  276.7 0.1 copy.80
  276.9 3.5 convolution_bitcast_fusion.1
  280.5 0.2 fusion.38
  280.8 0.8 copy.82
  281.6 213.6 %reduce-scatter.5.cloned.1.call-done = bf16[128,256]{1,0:T(8,128)(2,1)} async-done(((bf16[4096,256]{1,0:T(8,128)(2,1)}), bf16[128,256]{1,0:T(8,128)(2,1)}) %reduce-scatter.5.cloned.1.call-update) | async-done | bytes 65552 | tf_op jit(solution)/shard_map/reduce_scatter | solution.py:136
  495.2 0.8 convert_element_type.166
  496.1 0.9 fusion.55
  497.1 142.7 %all-reduce = (f32[640]{0:T(1024)}, f32[128]{0:T(128)}, f32[128]{0:T(128)}) all-reduce(f32[640]{0:T(1024)S(1)} %bitcast.185, f32[128]{0:T(128)S(1)} %get-tuple-element.24, f32[128]{0:T(128)S(1)} %get-tuple-element.36), channel_id=1, replica_groups=mesh['dp'=2,'ctx'=32,'tp'=8] {'dp','ctx'}, use_global_device_ids=true, to_apply=%region_8.9 | all-reduce | flops 896 | bytes 7168 | tf_op jit(solution)/shard_map/psum | solution.py:155
  639.8 0.6 fusion.51
  (39 shorter events, 0.8 us)
Async XLA Ops:
  7.2 10.3 %copy-start.7 = (f32[640]{0:T(1024)S(1)}, f32[640]{0:T(1024)}, u32[]{:S(2)}) copy-start(f32[640]{0:T(1024)} %param.13) | copy-start | bytes 7684
  7.2 9.9 %copy-start.8 = (s32[1,8]{1,0:T(1,128)S(1)}, s32[1,8]{1,0:T(1,128)}, u32[]{:S(2)}) copy-start(s32[1,8]{1,0:T(1,128)} %param.18) | copy-start | bytes 100
  7.2 93.2 %all-gather.8.cloned.1.call-start = ((), (), s32[]{:S(2)}) async-start(), calls=%async_computation.3 | async-start | bytes 1081344 | tf_op jit(solution)/shard_map/all_gather | solution.py:75
  11.0 130.9 %all-gather.12.cloned.1.call-start = ((), (), s32[]{:S(2)}) async-start(), calls=%async_computation.7 | async-start | bytes 1474560 | tf_op jit(solution)/shard_map/all_gather | solution.py:106
  11.8 159.1 %all-gather.10.cloned.1.call-start = ((), (), s32[]{:S(2)}) async-start(), calls=%async_computation.4 | async-start | bytes 9830400 | tf_op jit(solution)/shard_map/all_gather | solution.py:96
  12.5 244.8 %all-gather.6.cloned.1.call-start = ((), (), s32[]{:S(2)}) async-start(), calls=%async_computation.2 | async-start | bytes 1081344 | tf_op jit(solution)/shard_map/all_gather | solution.py:76
  14.8 480.3 %reduce-scatter.5.cloned.1.call-start = ((), (), s32[]{:S(2)}) async-start(), calls=%async_computation.6 | async-start | bytes 2162688 | tf_op jit(solution)/shard_map/reduce_scatter | solution.py:136
  16.1 84.3 %copy-start.2 = (bf16[1,128,640]{1,2,0:T(8,128)(2,1)}, bf16[1,128,640]{1,2,0:T(8,128)(2,1)S(1)}, u32[]{:S(2)}) copy-start(bf16[1,128,640]{1,2,0:T(8,128)(2,1)S(1)} %copy.64) | copy-start | bytes 491524
  257.3 3.9 copy-start.1
  261.2 6.5 %copy-start.3 = (bf16[1,128,640]{1,2,0:T(8,128)(2,1)S(1)}, bf16[1,128,640]{1,2,0:T(8,128)(2,1)}, u32[]{:S(2)}) copy-start(bf16[1,128,640]{1,2,0:T(8,128)(2,1)} %copy-done.2) | copy-start | bytes 491524
  265.4 2.4 copy-start
  271.3 369.2 %reduce-scatter.3.cloned.1.call-start = ((), (), s32[]{:S(2)}) async-start(), calls=%async_computation.5 | async-start | bytes 1474560 | tf_op jit(solution)/shard_map/reduce_scatter | solution.py:97
  271.3 5.3 copy-start.6
  271.3 5.4 copy-start.5
  271.3 5.5 copy-start.4
Sparse Core Ops, SparseCore 0:
  11.8 88.5 all-gather.7
  102.4 39.4 all-gather.11
  144.0 26.8 all-gather.9
  174.4 82.8 all-gather.5
  271.4 223.7 reduce-scatter.4
  498.7 39.8 reduce-scatter.2
where the time goes:
time: 658 us; the launch traced here: 647 us
  waiting for transfers between devices  433 us (66%)
  blocking collectives  143 us (22%)
  matrix products  30.9 us (5%)
  other arithmetic  19.1 us (3%)
  between operations  14.4 us (2%)
  local copies, waits for them, and re-layouts  6.68 us (1%)
    reduce_scatter x1, waiting for transfers between devices, shards(): lax.psum_scatter(jnp.concatenate([key_part.reshape(row_count * lax.axis_s...  214 us
    psum x1, blocking collectives, shards(): lax.psum((jnp.sum(pre_query, axis=0), jnp.sum(pre_key, axis=0), jnp.sum(g...  143 us
    all_gather x1, waiting for transfers between devices, shards(): lax.all_gather(key_row_block.reshape(row_count, k_width), 'ctx', axis=0,...  80.7 us
    all_gather x1, waiting for transfers between devices, shards(): lax.all_gather(value_row_block, 'ctx', axis=0, tiled=True)  76.6 us
    all_gather x1, waiting for transfers between devices, shards(): lax.all_gather(out_grad[0], 'tp', axis=0, tiled=True)  31.9 us
    all_gather x1, waiting for transfers between devices, shards(): full_weight = lax.all_gather(out_weight, 'dp', axis=1, tiled=True)  29 us
  transfers between devices with their start and end apart: 6, of which 5 were waited for; matrix products, arithmetic and copies ran while one was open for 6% of the time, Pallas kernels for 0%

commit v1 on v0

v1 whole, which is shorter than its diff:
```python
import functools

import jax
import jax.numpy as jnp
import numpy as np
from jax import lax
from jax.experimental import pallas as pl
from jax.experimental.pallas import tpu as pltpu
from jax.sharding import PartitionSpec as P

HW = 128
HALF = HW // 2
BLK = 64
ROPE_BASE = 1000000.0
NZ = 4
NZL = 2
CHUNK = 512
LOW = -1e30
LOG2E = 1.4426950408889634
MESH = pl.DeviceIdType.MESH
F32 = jnp.float32
BF16 = jnp.bfloat16
NT = (((1,), (1,)), ((), ()))
TN = (((0,), (0,)), ((), ()))


def dot(a, b):
    return jnp.dot(a, b, preferred_element_type=F32)


def turn(x):
    return pltpu.roll(x, HALF, 1)


class Wires:
    def __init__(self, send, recv):
        self.send, self.recv, self.all = send, recv, []

    def start(self, src, dst, target):
        n = len(self.all)
        copy = pltpu.make_async_remote_copy(
            src_ref=src,
            dst_ref=dst,
            send_sem=self.send.at[n],
            recv_sem=self.recv.at[n],
            device_id=target,
            device_id_type=MESH,
        )
        copy.start()
        self.all.append(copy)
        return copy

    def finish(self):
        for copy in self.all:
            copy.wait_send()


def kernel(
    dims,
    q_ref, k_ref, v_ref, qb_ref, kbias_ref, vbias_ref, freq_ref, bp_ref, doc_ref, w_hbm, og_hbm,
    out_ref, qg_ref, kg_ref, vg_ref, bias_ref,
    qn, qt, kb, vb, sb, eb, wb, og, dot_t, dot_n, o_rows, acc_o, acc_q, acc_g,
    pk, pv, rk_half, rk_full, rk_z, rv_half, rv_full, rv_z,
    po, rx_half, rx_full, rz, zs, mb, lb, ub, bpv, vs, btile, b_dp, b_z, b_y,
    local_sem, send_sem, recv_sem,
):
    NY, NX, G = dims
    ctx, tp, dp = lax.axis_index("ctx"), lax.axis_index("tp"), lax.axis_index("dp")
    z, y = ctx // NY, lax.rem(ctx, NY)
    zl, x = tp // NX, lax.rem(tp, NX)
    HY, HX = NY // 2, NX // 2
    QN = G * HW
    SUBS = NZ // 2
    ROWS = 4 * BLK

    def y_peer(d):
        return {"ctx": z * NY + lax.rem(y + d + NY, NY)}

    def z_peer(d):
        return {"ctx": lax.rem(z + d, NZ) * NY + y}

    def x_peer(d):
        return {"tp": zl * NX + lax.rem(x + d + NX, NX)}

    zl_peer = {"tp": (1 - zl) * NX + x}
    dp_peer = {"dp": 1 - dp}

    barrier = pltpu.get_barrier_semaphore()
    peers = [y_peer(d) for d in range(1, NY)] + [z_peer(d) for d in range(1, NZ)]
    peers += [x_peer(1), x_peer(-1), zl_peer, dp_peer]
    for peer in peers:
        pl.semaphore_signal(barrier, inc=1, device_id=peer, device_id_type=MESH)

    own_w = pltpu.make_async_copy(w_hbm, wb.at[dp], local_sem.at[0])
    own_w.start()
    own_g = pltpu.make_async_copy(og_hbm, og.at[tp], local_sem.at[1])
    own_g.start()

    b0, b1 = bp_ref[0, ctx, 0] * BLK, bp_ref[0, ctx, 1] * BLK
    sub = lax.broadcasted_iota(jnp.int32, (HW, HW), 0)
    pos = jnp.where(sub < BLK, b0 + sub, b1 + (sub - BLK))
    freq = freq_ref[...]
    angle = pos.astype(F32) * freq
    sign = jnp.where(lax.broadcasted_iota(jnp.int32, (1, HW), 1) < HALF, -1.0, 1.0)
    cos, sin = jnp.cos(angle), jnp.sin(angle) * sign
    inner = lax.broadcasted_iota(jnp.int32, (BLK, HW), 0).astype(F32) * freq
    cos_i, sin_i = jnp.cos(inner), jnp.sin(inner) * sign

    xk = k_ref[0].astype(F32) + kbias_ref[...]
    kb[0, 0] = (xk * cos + turn(xk) * sin).astype(BF16)
    vb[0, 0] = (v_ref[0].astype(F32) + vbias_ref[...]).astype(BF16)

    pl.semaphore_wait(barrier, len(peers))
    wires = Wires(send_sem, recv_sem)

    k_z = [wires.start(kb.at[0, 0], kb.at[0, r], z_peer(NZ - r)) for r in range(1, NZ)]
    g_x = [wires.start(og_hbm, og.at[tp], x_peer(d)) for d in (1, -1)]
    g_z = wires.start(og_hbm, og.at[tp], zl_peer)
    v_z = [wires.start(vb.at[0, 0], vb.at[0, r], z_peer(NZ - r)) for r in range(1, NZ)]
    far_w = wires.start(w_hbm, wb.at[dp], dp_peer)

    def gather_step(buf, k):
        if k < HY:
            up = wires.start(buf.at[(NY - (k - 1)) % NY], buf.at[NY - k], y_peer(1))
            down = wires.start(buf.at[k - 1], buf.at[k], y_peer(-1))
        else:
            lower, upper = pl.ds(0, NZ // 2), pl.ds(NZ // 2, NZ // 2)
            up = wires.start(buf.at[NY - k + 1, lower], buf.at[k, lower], y_peer(1))
            down = wires.start(buf.at[k - 1, upper], buf.at[k, upper], y_peer(-1))
        return [up, down]

    def arrived(copies):
        for copy in copies:
            copy.wait_recv()

    for h in range(G):
        cols = slice(h * HW, (h + 1) * HW)
        xq = q_ref[0, :, cols].astype(F32) + qb_ref[:, cols]
        rq = xq * cos + turn(xq) * sin
        qn[cols, :] = rq.astype(BF16)
        qt[:, cols] = rq.T.astype(BF16)
    lane = lax.broadcasted_iota(jnp.int32, (1, HW), 1)
    row_pos = jnp.where(lane < BLK, b0 + lane, b1 + (lane - BLK))
    end = jnp.int32(0)
    row_start = jnp.zeros((1, HW), jnp.int32)
    for d in range(doc_ref.shape[1]):
        row_start = jnp.where(row_pos >= end, end, row_start)
        end = end + doc_ref[0, d]
    row_pos = jnp.concatenate([row_pos] * G, axis=1)
    row_start = jnp.concatenate([row_start] * G, axis=1)
    mb[...] = jnp.full(mb.shape, LOW, F32)
    lb[...] = jnp.zeros(lb.shape, F32)
    vs[...] = jnp.zeros(vs.shape, F32)
    acc_o[...] = jnp.zeros(acc_o.shape, F32)
    acc_q[...] = jnp.zeros(acc_q.shape, F32)
    acc_g[...] = jnp.zeros(acc_g.shape, F32)

    def block_row(c, r):
        return lax.rem(z + r, NZ) * NY + lax.rem(y + c, NY)

    def base_step(i, carry):
        for h in range(2):
            bpv[pl.ds(2 * i + h, 1), :] = jnp.full((1, HW), bp_ref[0, i, h] * BLK, jnp.int32)
        return carry

    lax.fori_loop(0, NZ * NY, base_step, 0)

    def over(chunks, body):
        def step(i, carry):
            if len(chunks) == 1:
                c = chunks[0]
            else:
                c = chunks[0] + (i // SUBS) * (chunks[1] - chunks[0])
            body(c, lax.rem(i, SUBS))
            return carry

        lax.fori_loop(0, len(chunks) * SUBS, step, 0)

    def part_of(ref, c, p):
        return ref[c, pl.ds(2 * p, 2)].reshape(ROWS, HW)

    def score(c, p):
        s = dot(part_of(kb, c, p), qt[...])
        spot = lax.broadcasted_iota(jnp.int32, (BLK, QN), 0)
        most = mb[...]
        for j in range(4):
            base = bp_ref[0, block_row(c, 2 * p + j // 2), j % 2] * BLK
            piece = s[j * BLK:(j + 1) * BLK]
            piece = jnp.where((spot <= row_pos - base) & (spot >= row_start - base), piece, LOW)
            sb[c, p, j * BLK:(j + 1) * BLK, :] = piece
            most = jnp.maximum(most, jnp.max(piece.reshape(BLK // 8, 8, QN), axis=0))
        mb[...] = most

    def chunks_at(k):
        return [0] if k == 0 else [HY] if k == HY else [k, NY - k]

    arrived(k_z)
    k_y = {1: gather_step(kb, 1)}
    v_y = {}
    over(chunks_at(0), score)
    arrived(v_z)

    w_cols = wb.shape[2]
    left, right = pl.ds(0, w_cols), pl.ds(w_cols, w_cols)
    g_half = []
    g_next, g_last = [], []

    def opposite(line):
        from_left = zl_line(line) + lax.rem(x + NX - 1, NX)
        from_right = zl_line(line) + lax.rem(x + 1, NX)
        return [
            wires.start(og.at[from_left, :, left], og.at[from_left, :, left], x_peer(1)),
            wires.start(og.at[from_right, :, right], og.at[from_right, :, right], x_peer(-1)),
        ]

    def zl_line(line):
        return (zl if line == 0 else 1 - zl) * NX

    for k in range(1, HY):
        arrived(k_y[k])
        k_y[k + 1] = gather_step(kb, k + 1)
        if k > 1:
            arrived(v_y[k - 1])
        v_y[k] = gather_step(vb, k)
        if k == 1:
            arrived(g_x)
            g_half = opposite(0)
            g_z.wait_recv()
            partner = zl_line(1) + x
            g_next = [wires.start(og.at[partner], og.at[partner], x_peer(d)) for d in (1, -1)]
        over(chunks_at(k), score)
        if k == HY - 1:
            arrived(g_next)
            g_last = opposite(1)

    own_g.wait()
    own_w.wait()
    arrived(g_half)
    arrived(g_last)
    n_inner = w_cols // CHUNK

    def project(half):
        def step(n, carry):
            w = wb[half, :, pl.ds(pl.multiple_of(n * CHUNK, CHUNK), CHUNK)]
            at = pl.multiple_of(half * w_cols + n * CHUNK, CHUNK)
            g = og[:, :, pl.ds(at, CHUNK)].reshape(HW, CHUNK)
            acc_g[...] += lax.dot_general(w, g, NT, preferred_element_type=F32)
            return carry

        lax.fori_loop(0, n_inner, step, 0)

    project(dp)
    arrived(v_y[HY - 1])
    v_y[HY] = gather_step(vb, HY)
    far_w.wait_recv()
    project(1 - dp)
    for h in range(G):
        dot_t[:, h * HW:(h + 1) * HW] = acc_g[h * HW:(h + 1) * HW, :].astype(BF16)

    arrived(k_y[HY])
    over(chunks_at(HY), score)

    scale = HW ** -0.5
    top = jnp.max(mb[...], axis=0, keepdims=True) * (scale * LOG2E)

    def soften(i, carry):
        c, p = i // SUBS, lax.rem(i, SUBS)
        total = lb[...]
        for j in range(4):
            rows = slice(j * BLK, (j + 1) * BLK)
            e = jnp.exp2(sb[c, p, rows, :] * (scale * LOG2E) - top)
            total = total + jnp.sum(e.reshape(BLK // 8, 8, QN), axis=0)
            eb[c, p, rows, :] = e.astype(BF16)
        lb[...] = total
        return carry

    lax.fori_loop(0, NY * SUBS, soften, 0)
    inv = 1.0 / jnp.sum(lb[...], axis=0, keepdims=True)
    for h in range(G):
        cols = slice(h * HW, (h + 1) * HW)
        scaled = dot_t[:, cols].astype(F32) * inv[:, cols]
        dot_n[cols, :] = scaled.T.astype(BF16)

    def value_grad(c, p):
        g = dot(eb[c, p], dot_n[...])
        vs[...] += jnp.sum(g.reshape(ROWS // 8, 8, HW), axis=0)
        pv[c, pl.ds(2 * p, 2)] = g.astype(BF16).reshape(2, HW, HW)

    def attend(i, carry):
        c, p = i // SUBS, lax.rem(i, SUBS)
        acc_o[...] += lax.dot_general(part_of(vb, c, p), eb[c, p], TN, preferred_element_type=F32)
        return carry

    def scatter_step(buf, half, full, k):
        if k == 0:
            lower, upper = pl.ds(0, NZ // 2), pl.ds(NZ // 2, NZ // 2)
            up = wires.start(buf.at[HY, lower], half.at[0], y_peer(1))
            down = wires.start(buf.at[HY, upper], half.at[1], y_peer(-1))
        else:
            up = wires.start(buf.at[HY - k], full.at[k - 1, 0], y_peer(1))
            down = wires.start(buf.at[HY + k], full.at[k - 1, 1], y_peer(-1))
        return [up, down]

    def take(buf, half, full, k, copies):
        arrived(copies)
        if k == 0:
            for c, rows, i in ((HY - 1, slice(0, NZ // 2), 0), (HY + 1, slice(NZ // 2, NZ), 1)):
                buf[c, rows] = (buf[c, rows].astype(F32) + half[i].astype(F32)).astype(BF16)
        elif k < HY - 1:
            for c, i in ((HY - 1 - k, 0), (HY + 1 + k, 1)):
                buf[c] = (buf[c].astype(F32) + full[k - 1, i].astype(F32)).astype(BF16)
        else:
            both = full[k - 1, 0].astype(F32) + full[k - 1, 1].astype(F32)
            buf[0] = (buf[0].astype(F32) + both).astype(BF16)

    v_bufs, k_bufs = (pv, rv_half, rv_full), (pk, rk_half, rk_full)

    over(chunks_at(HY), value_grad)
    v_r = scatter_step(*v_bufs, 0)
    over(chunks_at(HY - 1), value_grad)
    arrived(v_y[HY])
    take(*v_bufs, 0, v_r)
    v_r = scatter_step(*v_bufs, 1)
    lax.fori_loop(0, NY * SUBS, attend, 0)
    o_t = (acc_o[...] * inv).astype(BF16)
    delta = jnp.sum(o_t.astype(F32) * dot_t[...].astype(F32), axis=0, keepdims=True) * inv
    for h in range(G):
        cols = slice(h * HW, (h + 1) * HW)
        o_rows[:, cols] = o_t[:, cols].astype(F32).T.astype(BF16)

    def key_grad(c, p):
        gp = dot(part_of(vb, c, p), dot_t[...])
        gs = (eb[c, p].astype(F32) * (gp * inv - delta)).astype(BF16)
        acc_q[...] += lax.dot_general(part_of(kb, c, p), gs, TN, preferred_element_type=F32)
        g = dot(gs, qn[...]) * scale
        pk[c, pl.ds(2 * p, 2)] = g.astype(BF16).reshape(2, HW, HW)
        for j in range(4):
            t = g[j * BLK:(j + 1) * BLK]
            back = t * cos_i - turn(t) * sin_i
            row = block_row(c, 2 * p + j // 2) * 2 + j % 2
            ub[pl.ds(row, 1), :] = jnp.sum(back, axis=0, keepdims=True)

    over(chunks_at(HY), key_grad)
    k_r = scatter_step(*k_bufs, 0)

    def mix(n, carry):
        half = n // n_inner
        at = pl.multiple_of(lax.rem(n, n_inner) * CHUNK, CHUNK)
        r = dot(o_rows[...], wb[half, :, pl.ds(at, CHUNK)]).astype(BF16)
        to = pl.multiple_of(n * CHUNK, CHUNK)
        po[:, :, :, pl.ds(to, CHUNK)] = r.reshape(NZL, NX, HW // (NZL * NX), CHUNK)
        return carry

    x_far, x_up, x_down = (lax.rem(x + d, NX) for d in (HX, 1, NX - 1))

    for k in range(1, HY):
        if k < HY - 1:
            over(chunks_at(HY - 1 - k), value_grad)
            take(*v_bufs, k, v_r)
            v_r = scatter_step(*v_bufs, k + 1)
        if k == 1:
            lax.fori_loop(0, 2 * n_inner, mix, 0)
            o_far = [
                wires.start(po.at[:, x_far, :, left], rx_half.at[0], x_peer(1)),
                wires.start(po.at[:, x_far, :, right], rx_half.at[1], x_peer(-1)),
            ]
        over(chunks_at(HY - k), key_grad)
        take(*k_bufs, k - 1, k_r)
        k_r = scatter_step(*k_bufs, k)
        if k == 2 or HY == 2:
            arrived(o_far)
            po[:, x_up, :, left] = (po[:, x_up, :, left].astype(F32) + rx_half[0].astype(F32)).astype(BF16)
            po[:, x_down, :, right] = (po[:, x_down, :, right].astype(F32) + rx_half[1].astype(F32)).astype(BF16)
            o_near = [
                wires.start(po.at[:, x_up], rx_full.at[0], x_peer(1)),
                wires.start(po.at[:, x_down], rx_full.at[1], x_peer(-1)),
            ]
    over(chunks_at(0), value_grad)
    over(chunks_at(0), key_grad)

    take(*v_bufs, HY - 1, v_r)
    v_zr = [wires.start(pv.at[0, r], rv_z.at[r - 1], z_peer(r)) for r in range(1, NZ)]

    for h in range(G):
        cols = slice(h * HW, (h + 1) * HW)
        g = acc_q[:, cols].T * scale
        g = g * cos - turn(g) * sin
        qg_ref[0, :, cols] = g.astype(BF16)
        btile[0, h:h + 1, :] = jnp.sum(g, axis=0, keepdims=True)
    base_angle = bpv[...].astype(F32) * freq
    u = ub[...]
    u = u * jnp.cos(base_angle) - turn(u) * (jnp.sin(base_angle) * sign)
    btile[0, G:G + 1, :] = jnp.sum(u, axis=0, keepdims=True)
    btile[0, G + 1:G + 2, :] = jnp.sum(vs[...], axis=0, keepdims=True)
    btile[0, G + 2:8, :] = jnp.zeros((8 - G - 2, HW), F32)
    bias_dp = wires.start(btile.at[0], b_dp, dp_peer)

    take(*k_bufs, HY - 1, k_r)
    k_zr = [wires.start(pk.at[0, r], rk_z.at[r - 1], z_peer(r)) for r in range(1, NZ)]

    bias_dp.wait_recv()
    btile[1] = btile[0] + b_dp[...]
    bias_z = [wires.start(btile.at[1], b_z.at[r - 1], z_peer(r)) for r in range(1, NZ)]

    arrived(o_near)
    other = 1 - zl
    zs[...] = (
        po[other, x].astype(F32) + rx_full[0, other].astype(F32) + rx_full[1, other].astype(F32)
    ).astype(BF16)
    o_z = wires.start(zs, rz, zl_peer)

    arrived(bias_z)
    total = btile[1]
    for r in range(NZ - 1):
        total = total + b_z[r]
    btile[2] = total
    bias_y = [wires.start(btile.at[2], b_y.at[d - 1], y_peer(d)) for d in range(1, NY)]

    arrived(v_zr)
    g = pv[0, 0].astype(F32)
    for r in range(NZ - 1):
        g = g + rv_z[r].astype(F32)
    vg_ref[0] = g.astype(BF16)

    o_z.wait_recv()
    out_ref[0] = (
        po[zl, x].astype(F32)
        + rx_full[0, zl].astype(F32)
        + rx_full[1, zl].astype(F32)
        + rz[...].astype(F32)
    ).astype(BF16)

    arrived(k_zr)
    g = pk[0, 0].astype(F32)
    for r in range(NZ - 1):
        g = g + rk_z[r].astype(F32)
    kg_ref[0] = (g * cos - turn(g) * sin).astype(BF16)

    arrived(bias_y)
    for d in range(NY - 1):
        total = total + b_y[d]
    bias_ref[...] = total
    wires.finish()


def layer(mesh_shape, q_in, key_input, value_input, q_bias, key_bias, value_bias, out_weight, out_grad, doc_lengths, block_pos):
    NY, NX = mesh_shape["ctx"] // NZ, mesh_shape["tp"] // NZL
    rows, features = q_in.shape[1:]
    G = features // HW
    own_rows, width = out_grad.shape[1:]
    w_cols = out_weight.shape[1]
    QN = G * HW
    SUBS, ROWS = NZ // 2, 4 * BLK
    freq = ROPE_BASE ** (-np.arange(0, HW, 2, dtype=np.float64) / HW)
    freq = jnp.asarray(np.concatenate([freq, freq])[None].astype(np.float32))
    vmem, anywhere = pl.BlockSpec(memory_space=pltpu.VMEM), pl.BlockSpec(memory_space=pl.ANY)
    smem = pl.BlockSpec(memory_space=pltpu.SMEM)
    V = pltpu.VMEM
    HY = NY // 2
    ring = [V((2, NZ // 2, HW, HW), BF16), V((HY - 1, 2, NZ, HW, HW), BF16), V((NZ - 1, HW, HW), BF16)]
    copies = 2 * (NZ - 1 + 2 * HY) + 1 + 9 + 2 * (2 * HY + NZ - 1) + 5 + 1 + NZ - 1 + NY - 1
    outs = pl.pallas_call(
        functools.partial(kernel, (NY, NX, G)),
        out_shape=(
            jax.ShapeDtypeStruct((1, own_rows, width), BF16),
            jax.ShapeDtypeStruct((1, rows, features), BF16),
            jax.ShapeDtypeStruct((1, rows, HW), BF16),
            jax.ShapeDtypeStruct((1, rows, HW), BF16),
            jax.ShapeDtypeStruct((8, HW), F32),
        ),
        in_specs=[vmem] * 7 + [smem] * 2 + [anywhere] * 2,
        out_specs=(vmem,) * 5,
        scratch_shapes=[
            V((QN, HW), BF16),
            V((HW, QN), BF16),
            V((NY, NZ, HW, HW), BF16),
            V((NY, NZ, HW, HW), BF16),
            V((NY, SUBS, ROWS, QN), F32),
            V((NY, SUBS, ROWS, QN), BF16),
            V((2, features, w_cols), BF16),
            V((NZL * NX, own_rows, width), BF16),
            V((HW, QN), BF16),
            V((QN, HW), BF16),
            V((HW, QN), BF16),
            V((HW, QN), F32),
            V((HW, QN), F32),
            V((QN, HW), F32),
            V((NY, NZ, HW, HW), BF16),
            V((NY, NZ, HW, HW), BF16),
            *ring,
            *ring,
            V((NZL, NX, own_rows, width), BF16),
            V((2, NZL, own_rows, w_cols), BF16),
            V((2, NZL, own_rows, width), BF16),
            V((own_rows, width), BF16),
            V((own_rows, width), BF16),
            V((8, QN), F32),
            V((8, QN), F32),
            V((2 * NZ * NY, HW), F32),
            V((2 * NZ * NY, HW), jnp.int32),
            V((8, HW), F32),
            V((3, 8, HW), F32),
            V((8, HW), F32),
            V((NZ - 1, 8, HW), F32),
            V((NY - 1, 8, HW), F32),
            pltpu.SemaphoreType.DMA((2,)),
            pltpu.SemaphoreType.DMA((copies,)),
            pltpu.SemaphoreType.DMA((copies,)),
        ],
        compiler_params=pltpu.CompilerParams(
            collective_id=0, has_side_effects=True, vmem_limit_bytes=60 * 1024 * 1024
        ),
        name="attention_layer",
    )(
        q_in, key_input, value_input, q_bias.reshape(1, -1), key_bias.reshape(1, -1),
        value_bias.reshape(1, -1), freq, block_pos, doc_lengths, out_weight, out_grad[0],
    )
    out, q_grad, k_grad, v_grad, bias = outs
    return (out, q_grad, k_grad, v_grad, bias[:G].reshape(-1), bias[G], bias[G + 1])


def solution(mesh):
    return jax.shard_map(
        functools.partial(layer, dict(mesh.shape)),
        mesh=mesh,
        in_specs=(
            P("dp", "ctx", "tp"),
            P("dp", "ctx", "tp"),
            P("dp", "ctx", "tp"),
            P("tp"),
            P("tp"),
            P("tp"),
            P("tp", "dp"),
            P("dp", ("ctx", "tp"), None),
            P("dp", None),
            P("dp", None, None),
        ),
        out_specs=(
            P("dp", ("ctx", "tp"), None),
            P("dp", "ctx", "tp"),
            P("dp", "ctx", "tp"),
            P("dp", "ctx", "tp"),
            P("tp"),
            P("tp"),
            P("tp"),
        ),
        check_vma=False,
    )
```

time: 658 us -> 109 us (0.17); the launches traced: 647 us -> 108 us
  waiting for transfers between devices: 433 us -> 0 us
  blocking collectives: 143 us -> 0 us
  Pallas kernels: 0 us -> 96.1 us
  matrix products: 30.9 us -> 0 us
  other arithmetic: 19.1 us -> 0 us
  between operations: 14.4 us -> 0.64 us
    all_gather x4 -> x0, waiting for transfers between devices: 218 us -> none  [the longest x1 80.7 us: shards(): lax.all_gather(key_row_block.reshape(row_count, k_width), 'ctx', axis=0,...]
    reduce_scatter x2 -> x0, waiting for transfers between devices: 214 us -> none  [the longest x1 214 us: shards(): lax.psum_scatter(jnp.concatenate([key_part.reshape(row_count * lax.axis_s...]
    psum x1 -> x0, blocking collectives: 143 us -> none  [shards(): lax.psum((jnp.sum(pre_query, axis=0), jnp.sum(pre_key, axis=0), jnp.sum(g...]
    pallas_call x0 -> x1, Pallas kernels: none -> 96.1 us  [layer(): pl.pallas_call(functools.partial(kernel, (NY, NX, G)), out_shape=(jax.Sha...]
    dot_general x8 -> x0, matrix products: 30.9 us -> none  [the longest x1 5.39 us: shards(): lax.dot_general(lax.all_gather(out_grad[0], 'tp', axis=0, tiled=True), fu...]
    convert_element_type x6 -> x0, other arithmetic: 7.78 us -> none  [the longest x1 4.61 us: shards(): jnp.exp(scores - (row_max + jnp.log(row_sum))).astype(jnp.bfloat16)]
  transfers between devices with their start and end apart: 6 -> 0, of which waited for: 5 -> 0; matrix products, arithmetic and copies ran while one was open for 6% -> 0% of each run, Pallas kernels for 0% -> 0%
where the time goes in v1:
time: 109 us; the launch traced here: 108 us
  Pallas kernels  96.1 us (88%)
  local copies, waits for them, and re-layouts  11.1 us (10%)
    pallas_call x1, Pallas kernels, layer(): pl.pallas_call(functools.partial(kernel, (NY, NX, G)), out_shape=(jax.Sha...  96.1 us
    unnamed x5, local copies, waits for them, and re-layouts  7.3 us

profile of v1, /device:TPU:6, one launch (start us, length us, event | category | flops | bytes accessed | tf_op | source)
XLA Modules:
  0.0 107.9 jit_solution(2389331925627570110)
XLA Ops:
  0.6 1.3 %reshape.26.qb_ref = f32[1,640]{1,0:T(1,128)} reshape(f32[640]{0:T(1024)} %param.14) | data formatting | bytes 5120 | tf_op jit(solution)/shard_map/reshape | solution.py:515
  1.9 1.4 %copy.18.bp_ref = s32[1,32,2]{2,1,0:T(8,128)} copy(s32[1,32,2]{1,2,0:T(2,128)} %param.20) | data formatting | bytes 512 | tf_op args[9]
  3.3 96.1 %attention_layer.1 = (bf16[1,16,5120]{2,1,0:T(8,128)(2,1)}, bf16[1,128,640]{2,1,0:T(8,128)(2,1)}, bf16[1,128,128]{2,1,0:T(8,128)(2,1)}, bf16[1,128,128]{2,1,0:T(8,128)(2,1)}, f32[8,128]{1,0:T(8,128)}) custom-call(bf16[1,128,640]{2,1,0:T(8,128)(2,1)} %q_ref.1, bf16[1,128,128]{2,1,0:T(8,128)(2,1)} %k_ref.1, bf16[1,128,128]{2,1,0:T(8,128)(2,1)} %v_ref.1, ...), custom_call_target="tpu_custom_call" | custom-call | tf_op jit(solution)/shard_map/attention_layer/pallas_call | solution.py:462
  99.4 1.3 %slice_bitcast_fusion = f32[640]{0:T(1024)} fusion(f32[8,128]{1,0:T(8,128)} %get-tuple-element.16), kind=kLoop, calls=%fused_computation | loop fusion | bytes 5120 | tf_op jit(solution)/shard_map/reshape | solution.py:519
  100.7 1.3 %slice_bitcast_fusion.1 = (f32[128]{0:T(128)}, f32[128]{0:T(128)}) fusion(f32[8,128]{1,0:T(8,128)} %get-tuple-element.16), kind=kLoop, calls=%fused_computation.1 | loop fusion | bytes 2048 | tf_op jit(solution)/shard_map/squeeze | solution.py:519
  101.9 1.6 %copy.23 = bf16[1,16,5120]{2,1,0:T(8,128)(2,1)} copy(bf16[1,16,5120]{2,1,0:T(8,128)(2,1)} %get-tuple-element.26) | data formatting | bytes 327680
  103.5 1.6 %copy.24 = bf16[1,128,640]{2,1,0:T(8,128)(2,1)} copy(bf16[1,128,640]{2,1,0:T(8,128)(2,1)} %get-tuple-element.27) | data formatting | bytes 327680
  105.1 1.4 %copy.25 = bf16[1,128,128]{2,1,0:T(8,128)(2,1)} copy(bf16[1,128,128]{2,1,0:T(8,128)(2,1)} %get-tuple-element.28) | data formatting | bytes 65536
  106.5 1.4 %copy.26 = bf16[1,128,128]{2,1,0:T(8,128)(2,1)} copy(bf16[1,128,128]{2,1,0:T(8,128)(2,1)} %get-tuple-element.29) | data formatting | bytes 65536

commit v2 on v1

--- a/solution.py
+++ b/solution.py
@@ -55,12 +55,18 @@
             copy.wait_send()
 
 
+class Term:
+    def __init__(self, buf, slots, landing):
+        self.buf, self.slots, self.landing = buf, slots, landing
+        self.out, self.last = {}, []
+
+
 def kernel(
     dims,
     q_ref, k_ref, v_ref, qb_ref, kbias_ref, vbias_ref, freq_ref, bp_ref, doc_ref, w_hbm, og_hbm,
     out_ref, qg_ref, kg_ref, vg_ref, bias_ref,
     qn, qt, kb, vb, sb, eb, wb, og, dot_t, dot_n, o_rows, acc_o, acc_q, acc_g,
-    pk, pv, rk_half, rk_full, rk_z, rv_half, rv_full, rv_z,
+    pk, pv, rk, rk_z, rv, rv_z,
     po, rx_half, rx_full, rz, zs, mb, lb, ub, bpv, vs, btile, b_dp, b_z, b_y,
     local_sem, send_sem, recv_sem,
 ):
@@ -70,8 +76,7 @@
     zl, x = tp // NX, lax.rem(tp, NX)
     HY, HX = NY // 2, NX // 2
     QN = G * HW
-    SUBS = NZ // 2
-    ROWS = 4 * BLK
+    ROWS = NZ * HW
 
     def y_peer(d):
         return {"ctx": z * NY + lax.rem(y + d + NY, NY)}
@@ -96,7 +101,7 @@
     own_g = pltpu.make_async_copy(og_hbm, og.at[tp], local_sem.at[1])
     own_g.start()
 
-    b0, b1 = bp_ref[0, ctx, 0] * BLK, bp_ref[0, ctx, 1] * BLK
+    b0, b1 = bp_ref[0, 0, ctx] * BLK, bp_ref[0, 1, ctx] * BLK
     sub = lax.broadcasted_iota(jnp.int32, (HW, HW), 0)
     pos = jnp.where(sub < BLK, b0 + sub, b1 + (sub - BLK))
     freq = freq_ref[...]
@@ -113,29 +118,41 @@
     pl.semaphore_wait(barrier, len(peers))
     wires = Wires(send_sem, recv_sem)
 
-    k_z = [wires.start(kb.at[0, 0], kb.at[0, r], z_peer(NZ - r)) for r in range(1, NZ)]
-    g_x = [wires.start(og_hbm, og.at[tp], x_peer(d)) for d in (1, -1)]
-    g_z = wires.start(og_hbm, og.at[tp], zl_peer)
-    v_z = [wires.start(vb.at[0, 0], vb.at[0, r], z_peer(NZ - r)) for r in range(1, NZ)]
-    far_w = wires.start(w_hbm, wb.at[dp], dp_peer)
-
-    def gather_step(buf, k):
-        if k < HY:
-            up = wires.start(buf.at[(NY - (k - 1)) % NY], buf.at[NY - k], y_peer(1))
-            down = wires.start(buf.at[k - 1], buf.at[k], y_peer(-1))
-        else:
-            lower, upper = pl.ds(0, NZ // 2), pl.ds(NZ // 2, NZ // 2)
-            up = wires.start(buf.at[NY - k + 1, lower], buf.at[k, lower], y_peer(1))
-            down = wires.start(buf.at[k - 1, upper], buf.at[k, upper], y_peer(-1))
-        return [up, down]
+    lower = range(NZ // 2)
+    order = [1, 3, 2][:NZ - 1] if NZ > 2 else [1]
 
     def arrived(copies):
         for copy in copies:
             copy.wait_recv()
 
+    def hop(buf, k, r):
+        last = k == HY
+        copies = []
+        if not last or r in lower:
+            copies.append(wires.start(buf.at[(NY - k + 1) % NY, r], buf.at[NY - k, r], y_peer(1)))
+        if not last or r not in lower:
+            copies.append(wires.start(buf.at[k - 1, r], buf.at[k, r], y_peer(-1)))
+        return copies
+
+    def forward(buf, seen, k, chains):
+        for r in chains:
+            arrived(seen[k, r])
+            seen[k + 1, r] = hop(buf, k + 1, r)
+
+    k_in, v_in = {}, {}
+    for r in order:
+        k_in[0, r] = [wires.start(kb.at[0, 0], kb.at[0, r], z_peer(NZ - r))]
+    k_in[1, 0] = hop(kb, 1, 0)
+    g_x = [wires.start(og_hbm, og.at[tp], x_peer(d)) for d in (1, -1)]
+    g_z = wires.start(og_hbm, og.at[tp], zl_peer)
+    for r in order:
+        v_in[0, r] = [wires.start(vb.at[0, 0], vb.at[0, r], z_peer(NZ - r))]
+    v_in[1, 0] = hop(vb, 1, 0)
+    far_w = wires.start(w_hbm, wb.at[dp], dp_peer)
+
     for h in range(G):
         cols = slice(h * HW, (h + 1) * HW)
-        xq = q_ref[0, :, cols].astype(F32) + qb_ref[:, cols]
+        xq = q_ref[0, :, cols].astype(F32) + qb_ref[cols][None, :]
         rq = xq * cos + turn(xq) * sin
         qn[cols, :] = rq.astype(BF16)
         qt[:, cols] = rq.T.astype(BF16)
@@ -160,50 +177,38 @@
 
     def base_step(i, carry):
         for h in range(2):
-            bpv[pl.ds(2 * i + h, 1), :] = jnp.full((1, HW), bp_ref[0, i, h] * BLK, jnp.int32)
+            bpv[pl.ds(2 * i + h, 1), :] = jnp.full((1, HW), bp_ref[0, h, i] * BLK, jnp.int32)
         return carry
 
     lax.fori_loop(0, NZ * NY, base_step, 0)
 
     def over(chunks, body):
         def step(i, carry):
-            if len(chunks) == 1:
-                c = chunks[0]
-            else:
-                c = chunks[0] + (i // SUBS) * (chunks[1] - chunks[0])
-            body(c, lax.rem(i, SUBS))
+            body(chunks[0] + i * (chunks[-1] - chunks[0]))
             return carry
 
-        lax.fori_loop(0, len(chunks) * SUBS, step, 0)
-
-    def part_of(ref, c, p):
-        return ref[c, pl.ds(2 * p, 2)].reshape(ROWS, HW)
-
-    def score(c, p):
-        s = dot(part_of(kb, c, p), qt[...])
+        lax.fori_loop(0, len(chunks), step, 0)
+
+    def whole(ref, c):
+        return ref[c].reshape(ROWS, HW)
+
+    def score(c):
+        s = dot(whole(kb, c), qt[...])
         spot = lax.broadcasted_iota(jnp.int32, (BLK, QN), 0)
         most = mb[...]
-        for j in range(4):
-            base = bp_ref[0, block_row(c, 2 * p + j // 2), j % 2] * BLK
+        for j in range(2 * NZ):
+            base = bp_ref[0, j % 2, block_row(c, j // 2)] * BLK
             piece = s[j * BLK:(j + 1) * BLK]
             piece = jnp.where((spot <= row_pos - base) & (spot >= row_start - base), piece, LOW)
-            sb[c, p, j * BLK:(j + 1) * BLK, :] = piece
+            sb[c, j * BLK:(j + 1) * BLK, :] = piece
             most = jnp.maximum(most, jnp.max(piece.reshape(BLK // 8, 8, QN), axis=0))
         mb[...] = most
 
     def chunks_at(k):
         return [0] if k == 0 else [HY] if k == HY else [k, NY - k]
 
-    arrived(k_z)
-    k_y = {1: gather_step(kb, 1)}
-    v_y = {}
-    over(chunks_at(0), score)
-    arrived(v_z)
-
     w_cols = wb.shape[2]
     left, right = pl.ds(0, w_cols), pl.ds(w_cols, w_cols)
-    g_half = []
-    g_next, g_last = [], []
 
     def opposite(line):
         from_left = zl_line(line) + lax.rem(x + NX - 1, NX)
@@ -216,27 +221,32 @@
     def zl_line(line):
         return (zl if line == 0 else 1 - zl) * NX
 
+    own = [0]
+    forward(kb, k_in, 1, own)
+    forward(vb, v_in, 1, own)
+    forward(kb, k_in, 0, order)
+    arrived(g_x)
+    g_half = opposite(0)
+    if HY > 2:
+        forward(kb, k_in, 2, own)
+        forward(vb, v_in, 2, own)
+    over(chunks_at(0), score)
+    g_z.wait_recv()
+    partner = zl_line(1) + x
+    g_next = [wires.start(og.at[partner], og.at[partner], x_peer(d)) for d in (1, -1)]
+    if HY > 3:
+        forward(kb, k_in, 3, own)
+        forward(vb, v_in, 3, own)
     for k in range(1, HY):
-        arrived(k_y[k])
-        k_y[k + 1] = gather_step(kb, k + 1)
-        if k > 1:
-            arrived(v_y[k - 1])
-        v_y[k] = gather_step(vb, k)
-        if k == 1:
-            arrived(g_x)
-            g_half = opposite(0)
-            g_z.wait_recv()
-            partner = zl_line(1) + x
-            g_next = [wires.start(og.at[partner], og.at[partner], x_peer(d)) for d in (1, -1)]
+        forward(kb, k_in, k, order)
         over(chunks_at(k), score)
-        if k == HY - 1:
+        forward(vb, v_in, k - 1, order)
+        if k == 2 or HY == 2:
             arrived(g_next)
             g_last = opposite(1)
 
     own_g.wait()
     own_w.wait()
-    arrived(g_half)
-    arrived(g_last)
     n_inner = w_cols // CHUNK
 
     def project(half):
@@ -249,99 +259,115 @@
 
         lax.fori_loop(0, n_inner, step, 0)
 
+    arrived(g_half)
+    arrived(g_last)
     project(dp)
-    arrived(v_y[HY - 1])
-    v_y[HY] = gather_step(vb, HY)
     far_w.wait_recv()
     project(1 - dp)
     for h in range(G):
         dot_t[:, h * HW:(h + 1) * HW] = acc_g[h * HW:(h + 1) * HW, :].astype(BF16)
 
-    arrived(k_y[HY])
+    for r in range(NZ):
+        arrived(k_in[HY, r])
     over(chunks_at(HY), score)
+    forward(vb, v_in, HY - 1, order)
 
     scale = HW ** -0.5
     top = jnp.max(mb[...], axis=0, keepdims=True) * (scale * LOG2E)
 
-    def soften(i, carry):
-        c, p = i // SUBS, lax.rem(i, SUBS)
+    def soften(c, carry):
         total = lb[...]
-        for j in range(4):
+        for j in range(2 * NZ):
             rows = slice(j * BLK, (j + 1) * BLK)
-            e = jnp.exp2(sb[c, p, rows, :] * (scale * LOG2E) - top)
+            e = jnp.exp2(sb[c, rows, :] * (scale * LOG2E) - top)
             total = total + jnp.sum(e.reshape(BLK // 8, 8, QN), axis=0)
-            eb[c, p, rows, :] = e.astype(BF16)
+            eb[c, rows, :] = e.astype(BF16)
         lb[...] = total
         return carry
 
-    lax.fori_loop(0, NY * SUBS, soften, 0)
+    lax.fori_loop(0, NY, soften, 0)
     inv = 1.0 / jnp.sum(lb[...], axis=0, keepdims=True)
     for h in range(G):
         cols = slice(h * HW, (h + 1) * HW)
         scaled = dot_t[:, cols].astype(F32) * inv[:, cols]
         dot_n[cols, :] = scaled.T.astype(BF16)
 
-    def value_grad(c, p):
-        g = dot(eb[c, p], dot_n[...])
+    def value_grad(c):
+        g = dot(eb[c], dot_n[...])
         vs[...] += jnp.sum(g.reshape(ROWS // 8, 8, HW), axis=0)
-        pv[c, pl.ds(2 * p, 2)] = g.astype(BF16).reshape(2, HW, HW)
-
-    def attend(i, carry):
-        c, p = i // SUBS, lax.rem(i, SUBS)
-        acc_o[...] += lax.dot_general(part_of(vb, c, p), eb[c, p], TN, preferred_element_type=F32)
-        return carry
-
-    def scatter_step(buf, half, full, k):
-        if k == 0:
-            lower, upper = pl.ds(0, NZ // 2), pl.ds(NZ // 2, NZ // 2)
-            up = wires.start(buf.at[HY, lower], half.at[0], y_peer(1))
-            down = wires.start(buf.at[HY, upper], half.at[1], y_peer(-1))
-        else:
-            up = wires.start(buf.at[HY - k], full.at[k - 1, 0], y_peer(1))
-            down = wires.start(buf.at[HY + k], full.at[k - 1, 1], y_peer(-1))
-        return [up, down]
-
-    def take(buf, half, full, k, copies):
-        arrived(copies)
-        if k == 0:
-            for c, rows, i in ((HY - 1, slice(0, NZ // 2), 0), (HY + 1, slice(NZ // 2, NZ), 1)):
-                buf[c, rows] = (buf[c, rows].astype(F32) + half[i].astype(F32)).astype(BF16)
-        elif k < HY - 1:
-            for c, i in ((HY - 1 - k, 0), (HY + 1 + k, 1)):
-                buf[c] = (buf[c].astype(F32) + full[k - 1, i].astype(F32)).astype(BF16)
-        else:
-            both = full[k - 1, 0].astype(F32) + full[k - 1, 1].astype(F32)
-            buf[0] = (buf[0].astype(F32) + both).astype(BF16)
-
-    v_bufs, k_bufs = (pv, rv_half, rv_full), (pk, rk_half, rk_full)
+        pv[c] = g.astype(BF16).reshape(NZ, HW, HW)
+
+    def attend(c):
+        acc_o[...] += lax.dot_general(whole(vb, c), eb[c], TN, preferred_element_type=F32)
+
+    def send_terms(term, r, up, down, k):
+        if up:
+            term.out[k, r, 0] = wires.start(term.buf.at[HY - k, r], term.slots.at[k, 0, r], y_peer(1))
+        if down:
+            term.out[k, r, 1] = wires.start(term.buf.at[HY + k, r], term.slots.at[k, 1, r], y_peer(-1))
+
+    def scatter(term, k):
+        for r in range(NZ):
+            for way, c in ((0, HY - k), (1, HY + k)):
+                if (k - 1, r, way) in term.out:
+                    term.out[k - 1, r, way].wait_recv()
+                    term.buf[c, r] = (term.buf[c, r].astype(F32) + term.slots[k - 1, way, r].astype(F32)).astype(BF16)
+            send_terms(term, r, k > 0 or r in lower, k > 0 or r not in lower, k)
+
+    def settle(term):
+        for r in order + [0]:
+            arrived([term.out[HY - 1, r, way] for way in (0, 1)])
+            both = term.slots[HY - 1, 0, r].astype(F32) + term.slots[HY - 1, 1, r].astype(F32)
+            term.buf[0, r] = (term.buf[0, r].astype(F32) + both).astype(BF16)
+            if r:
+                term.last.append(wires.start(term.buf.at[0, r], term.landing.at[r - 1], z_peer(r)))
+
+    def total_of(term):
+        arrived(term.last)
+        g = term.buf[0, 0].astype(F32)
+        for r in range(NZ - 1):
+            g = g + term.landing[r].astype(F32)
+        return g
+
+    v_term, k_term = Term(pv, rv, rv_z), Term(pk, rk, rk_z)
 
     over(chunks_at(HY), value_grad)
-    v_r = scatter_step(*v_bufs, 0)
+    scatter(v_term, 0)
     over(chunks_at(HY - 1), value_grad)
-    arrived(v_y[HY])
-    take(*v_bufs, 0, v_r)
-    v_r = scatter_step(*v_bufs, 1)
-    lax.fori_loop(0, NY * SUBS, attend, 0)
+    scatter(v_term, 1)
+    if HY > 2:
+        over(chunks_at(HY - 2), value_grad)
+    for k in range(HY):
+        over(chunks_at(k), attend)
+    if HY > 2:
+        scatter(v_term, 2)
+    for k in range(1, HY - 2):
+        over(chunks_at(k), value_grad)
+    for r in range(NZ):
+        arrived(v_in[HY, r])
+    over(chunks_at(HY), attend)
     o_t = (acc_o[...] * inv).astype(BF16)
     delta = jnp.sum(o_t.astype(F32) * dot_t[...].astype(F32), axis=0, keepdims=True) * inv
     for h in range(G):
         cols = slice(h * HW, (h + 1) * HW)
         o_rows[:, cols] = o_t[:, cols].astype(F32).T.astype(BF16)
 
-    def key_grad(c, p):
-        gp = dot(part_of(vb, c, p), dot_t[...])
-        gs = (eb[c, p].astype(F32) * (gp * inv - delta)).astype(BF16)
-        acc_q[...] += lax.dot_general(part_of(kb, c, p), gs, TN, preferred_element_type=F32)
+    def key_grad(c):
+        gp = dot(whole(vb, c), dot_t[...])
+        gs = (eb[c].astype(F32) * (gp * inv - delta)).astype(BF16)
+        acc_q[...] += lax.dot_general(whole(kb, c), gs, TN, preferred_element_type=F32)
         g = dot(gs, qn[...]) * scale
-        pk[c, pl.ds(2 * p, 2)] = g.astype(BF16).reshape(2, HW, HW)
-        for j in range(4):
+        pk[c] = g.astype(BF16).reshape(NZ, HW, HW)
+        for j in range(2 * NZ):
             t = g[j * BLK:(j + 1) * BLK]
             back = t * cos_i - turn(t) * sin_i
-            row = block_row(c, 2 * p + j // 2) * 2 + j % 2
+            row = block_row(c, j // 2) * 2 + j % 2
             ub[pl.ds(row, 1), :] = jnp.sum(back, axis=0, keepdims=True)
 
     over(chunks_at(HY), key_grad)
-    k_r = scatter_step(*k_bufs, 0)
+    scatter(k_term, 0)
+    for k in range(3, HY):
+        scatter(v_term, k)
 
     def mix(n, carry):
         half = n // n_inner
@@ -353,20 +379,17 @@
 
     x_far, x_up, x_down = (lax.rem(x + d, NX) for d in (HX, 1, NX - 1))
 
+    lax.fori_loop(0, 2 * n_inner, mix, 0)
+    o_far = [
+        wires.start(po.at[:, x_far, :, left], rx_half.at[0], x_peer(1)),
+        wires.start(po.at[:, x_far, :, right], rx_half.at[1], x_peer(-1)),
+    ]
     for k in range(1, HY):
-        if k < HY - 1:
-            over(chunks_at(HY - 1 - k), value_grad)
-            take(*v_bufs, k, v_r)
-            v_r = scatter_step(*v_bufs, k + 1)
+        over(chunks_at(HY - k), key_grad)
+        scatter(k_term, k)
         if k == 1:
-            lax.fori_loop(0, 2 * n_inner, mix, 0)
-            o_far = [
-                wires.start(po.at[:, x_far, :, left], rx_half.at[0], x_peer(1)),
-                wires.start(po.at[:, x_far, :, right], rx_half.at[1], x_peer(-1)),
-            ]
-        over(chunks_at(HY - k), key_grad)
-        take(*k_bufs, k - 1, k_r)
-        k_r = scatter_step(*k_bufs, k)
+            over(chunks_at(0), value_grad)
+            settle(v_term)
         if k == 2 or HY == 2:
             arrived(o_far)
             po[:, x_up, :, left] = (po[:, x_up, :, left].astype(F32) + rx_half[0].astype(F32)).astype(BF16)
@@ -375,11 +398,7 @@
                 wires.start(po.at[:, x_up], rx_full.at[0], x_peer(1)),
                 wires.start(po.at[:, x_down], rx_full.at[1], x_peer(-1)),
             ]
-    over(chunks_at(0), value_grad)
     over(chunks_at(0), key_grad)
-
-    take(*v_bufs, HY - 1, v_r)
-    v_zr = [wires.start(pv.at[0, r], rv_z.at[r - 1], z_peer(r)) for r in range(1, NZ)]
 
     for h in range(G):
         cols = slice(h * HW, (h + 1) * HW)
@@ -395,8 +414,7 @@
     btile[0, G + 2:8, :] = jnp.zeros((8 - G - 2, HW), F32)
     bias_dp = wires.start(btile.at[0], b_dp, dp_peer)
 
-    take(*k_bufs, HY - 1, k_r)
-    k_zr = [wires.start(pk.at[0, r], rk_z.at[r - 1], z_peer(r)) for r in range(1, NZ)]
+    settle(k_term)
 
     bias_dp.wait_recv()
     btile[1] = btile[0] + b_dp[...]
@@ -416,11 +434,7 @@
     btile[2] = total
     bias_y = [wires.start(btile.at[2], b_y.at[d - 1], y_peer(d)) for d in range(1, NY)]
 
-    arrived(v_zr)
-    g = pv[0, 0].astype(F32)
-    for r in range(NZ - 1):
-        g = g + rv_z[r].astype(F32)
-    vg_ref[0] = g.astype(BF16)
+    vg_ref[0] = total_of(v_term).astype(BF16)
 
     o_z.wait_recv()
     out_ref[0] = (
@@ -430,10 +444,7 @@
         + rz[...].astype(F32)
     ).astype(BF16)
 
-    arrived(k_zr)
-    g = pk[0, 0].astype(F32)
-    for r in range(NZ - 1):
-        g = g + rk_z[r].astype(F32)
+    g = total_of(k_term)
     kg_ref[0] = (g * cos - turn(g) * sin).astype(BF16)
 
     arrived(bias_y)
@@ -450,15 +461,15 @@
     own_rows, width = out_grad.shape[1:]
     w_cols = out_weight.shape[1]
     QN = G * HW
-    SUBS, ROWS = NZ // 2, 4 * BLK
+    ROWS = NZ * HW
     freq = ROPE_BASE ** (-np.arange(0, HW, 2, dtype=np.float64) / HW)
     freq = jnp.asarray(np.concatenate([freq, freq])[None].astype(np.float32))
     vmem, anywhere = pl.BlockSpec(memory_space=pltpu.VMEM), pl.BlockSpec(memory_space=pl.ANY)
     smem = pl.BlockSpec(memory_space=pltpu.SMEM)
     V = pltpu.VMEM
     HY = NY // 2
-    ring = [V((2, NZ // 2, HW, HW), BF16), V((HY - 1, 2, NZ, HW, HW), BF16), V((NZ - 1, HW, HW), BF16)]
-    copies = 2 * (NZ - 1 + 2 * HY) + 1 + 9 + 2 * (2 * HY + NZ - 1) + 5 + 1 + NZ - 1 + NY - 1
+    ring = [V((HY, 2, NZ, HW, HW), BF16), V((NZ - 1, HW, HW), BF16)]
+    copies = 4 * (NZ - 1 + NZ * (2 * HY - 1)) + 16 + NZ + NY
     outs = pl.pallas_call(
         functools.partial(kernel, (NY, NX, G)),
         out_shape=(
@@ -475,8 +486,8 @@
             V((HW, QN), BF16),
             V((NY, NZ, HW, HW), BF16),
             V((NY, NZ, HW, HW), BF16),
-            V((NY, SUBS, ROWS, QN), F32),
-            V((NY, SUBS, ROWS, QN), BF16),
+            V((NY, ROWS, QN), F32),
+            V((NY, ROWS, QN), BF16),
             V((2, features, w_cols), BF16),
             V((NZL * NX, own_rows, width), BF16),
             V((HW, QN), BF16),
@@ -512,11 +523,29 @@
         ),
         name="attention_layer",
     )(
-        q_in, key_input, value_input, q_bias.reshape(1, -1), key_bias.reshape(1, -1),
-        value_bias.reshape(1, -1), freq, block_pos, doc_lengths, out_weight, out_grad[0],
+        q_in, key_input, value_input, q_bias, key_bias.reshape(1, -1),
+        value_bias.reshape(1, -1), freq, jnp.swapaxes(block_pos, 1, 2), doc_lengths, out_weight, out_grad[0],
     )
-    out, q_grad, k_grad, v_grad, bias = outs
-    return (out, q_grad, k_grad, v_grad, bias[:G].reshape(-1), bias[G], bias[G + 1])
+    shapes = [jax.ShapeDtypeStruct(o.shape, o.dtype) for o in outs[:4]]
+    shapes += [jax.ShapeDtypeStruct((n,), F32) for n in (features, HW, HW)]
+    return pl.pallas_call(
+        functools.partial(finish, G),
+        out_shape=tuple(shapes),
+        in_specs=[vmem] * 5,
+        out_specs=(vmem,) * 7,
+        compiler_params=pltpu.CompilerParams(vmem_limit_bytes=60 * 1024 * 1024),
+        name="hand_over",
+    )(*outs)
+
+
+def finish(G, *refs):
+    bias_ref, biases = refs[4], refs[9:]
+    for source, target in zip(refs[:4], refs[5:9]):
+        target[...] = source[...]
+    for h in range(G):
+        biases[0][h * HW:(h + 1) * HW] = bias_ref[h]
+    biases[1][...] = bias_ref[G]
+    biases[2][...] = bias_ref[G + 1]
 
 
 def solution(mesh):

time: 109 us -> 90 us (0.83)
  local copies, waits for them, and re-layouts: 11.1 us -> 0 us
  Pallas kernels: 96.1 us -> 88.3 us
    pallas_call x1, Pallas kernels: 96.1 us -> 86.5 us  [layer(): pl.pallas_call(functools.partial(kernel, (NY, NX, G)), out_shape=(jax.Sha...]
    unnamed x5 -> x0, local copies, waits for them, and re-layouts: 7.3 us -> none
    reshape x2 -> x0, local copies, waits for them, and re-layouts: 2.54 us -> none  [the longest x1 1.28 us: layer(): bias[:G].reshape(-1)]
    pallas_call x0 -> x1, Pallas kernels: none -> 1.78 us  [layer(): pl.pallas_call(functools.partial(finish, G), out_shape=tuple(shapes), in_...]
    squeeze x1 -> x0, local copies, waits for them, and re-layouts: 1.27 us -> none  [layer(): bias[G + 1]]
where the time goes in v2:
time: 90 us; the launch traced here: 89 us
  Pallas kernels  88.3 us (98%)
    pallas_call x1, Pallas kernels, layer(): pl.pallas_call(functools.partial(kernel, (NY, NX, G)), out_shape=(jax.Sha...  86.5 us

profile of v2, /device:TPU:6, one launch (start us, length us, event | category | flops | bytes accessed | tf_op | source)
XLA Modules:
  0.0 89.0 jit_solution(11065152882884384332)
XLA Ops:
  0.6 86.5 %attention_layer.1 = (bf16[1,16,5120]{2,1,0:T(8,128)(2,1)}, bf16[1,128,640]{2,1,0:T(8,128)(2,1)}, bf16[1,128,128]{2,1,0:T(8,128)(2,1)}, bf16[1,128,128]{2,1,0:T(8,128)(2,1)}, f32[8,128]{1,0:T(8,128)}) custom-call(bf16[1,128,640]{2,1,0:T(8,128)(2,1)} %q_ref.1, bf16[1,128,128]{2,1,0:T(8,128)(2,1)} %k_ref.1, bf16[1,128,128]{2,1,0:T(8,128)(2,1)} %v_ref.1, ...), custom_call_target="tpu_custom_call" | custom-call | tf_op jit(solution)/shard_map/attention_layer/pallas_call | solution.py:473
  87.2 1.8 %hand_over.1 = (bf16[1,16,5120]{2,1,0:T(8,128)(2,1)}, bf16[1,128,640]{2,1,0:T(8,128)(2,1)}, bf16[1,128,128]{2,1,0:T(8,128)(2,1)}, bf16[1,128,128]{2,1,0:T(8,128)...) custom-call(bf16[1,16,5120]{2,1,0:T(8,128)(2,1)} %get-tuple-element.12.refs_0_, ...), custom_call_target="tpu_custom_call" | custom-call | tf_op jit(solution)/shard_map/hand_over/pallas_call | solution.py:531

commit v3 on v2

--- a/solution.py
+++ b/solution.py
@@ -55,6 +55,24 @@
             copy.wait_send()
 
 
+def near_and_far(n):
+    away = [[n // 2]] + [[d, n - d] for d in range(n // 2 - 1, 0, -1)]
+    near = [c for pair in away for c in pair if pair[0] <= n // 4]
+    return near, [c for pair in away for c in pair if pair[0] > n // 4]
+
+
+def pairs(chunks):
+    odd = len(chunks) % 2
+    return [chunks[:1]] * odd + [chunks[i:i + 2] for i in range(odd, len(chunks), 2)]
+
+
+class Direct:
+    def __init__(self, buf, slots, far_slots, middle, landing):
+        self.buf, self.slots, self.far_slots = buf, slots, far_slots
+        self.middle, self.landing = middle, landing
+        self.first, self.direct, self.last = {}, [], []
+
+
 class Term:
     def __init__(self, buf, slots, landing):
         self.buf, self.slots, self.landing = buf, slots, landing
@@ -66,7 +84,7 @@
     q_ref, k_ref, v_ref, qb_ref, kbias_ref, vbias_ref, freq_ref, bp_ref, doc_ref, w_hbm, og_hbm,
     out_ref, qg_ref, kg_ref, vg_ref, bias_ref,
     qn, qt, kb, vb, sb, eb, wb, og, dot_t, dot_n, o_rows, acc_o, acc_q, acc_g,
-    pk, pv, rk, rk_z, rv, rv_z,
+    pk, pv, rk, rk_f, rk_m, rk_z, rv, rv_z,
     po, rx_half, rx_full, rz, zs, mb, lb, ub, bpv, vs, btile, b_dp, b_z, b_y,
     local_sem, send_sem, recv_sem,
 ):
@@ -120,6 +138,7 @@
 
     lower = range(NZ // 2)
     order = [1, 3, 2][:NZ - 1] if NZ > 2 else [1]
+    near, far = near_and_far(NY)
 
     def arrived(copies):
         for copy in copies:
@@ -270,7 +289,6 @@
     for r in range(NZ):
         arrived(k_in[HY, r])
     over(chunks_at(HY), score)
-    forward(vb, v_in, HY - 1, order)
 
     scale = HW ** -0.5
     top = jnp.max(mb[...], axis=0, keepdims=True) * (scale * LOG2E)
@@ -329,10 +347,49 @@
             g = g + term.landing[r].astype(F32)
         return g
 
-    v_term, k_term = Term(pv, rv, rv_z), Term(pk, rk, rk_z)
+    def send_far(term, chunks):
+        for c in chunks:
+            for r in order[::-1]:
+                term.first[c, r] = wires.start(term.buf.at[c, r], term.middle.at[far.index(c), r - 1], z_peer(r))
+
+    def send_near(term, chunks):
+        for c in chunks:
+            term.direct.append(wires.start(term.buf.at[c], term.slots.at[near.index(c)], y_peer(c)))
+
+    def pass_on(term):
+        for c in far:
+            g = term.buf[c, 0].astype(F32)
+            for r in order[::-1]:
+                term.first[c, r].wait_recv()
+                g = g + term.middle[far.index(c), r - 1].astype(F32)
+            term.buf[c, 0] = g.astype(BF16)
+            term.last.append(wires.start(term.buf.at[c, 0], term.far_slots.at[far.index(c)], y_peer(c)))
+
+    def finish_near(term):
+        arrived(term.direct)
+        for r in order[::-1]:
+            g = term.buf[0, r].astype(F32)
+            for i in range(len(near)):
+                g = g + term.slots[i, r].astype(F32)
+            term.buf[0, r] = g.astype(BF16)
+            term.last.append(wires.start(term.buf.at[0, r], term.landing.at[r - 1], z_peer(r)))
+
+    def whole_of(term):
+        arrived(term.last)
+        g = term.buf[0, 0].astype(F32)
+        for i in range(len(near)):
+            g = g + term.slots[i, 0].astype(F32)
+        for i in range(len(far)):
+            g = g + term.far_slots[i].astype(F32)
+        for r in range(NZ - 1):
+            g = g + term.landing[r].astype(F32)
+        return g
+
+    v_term, k_term = Term(pv, rv, rv_z), Direct(pk, rk, rk_f, rk_m, rk_z)
 
     over(chunks_at(HY), value_grad)
     scatter(v_term, 0)
+    forward(vb, v_in, HY - 1, order)
     over(chunks_at(HY - 1), value_grad)
     scatter(v_term, 1)
     if HY > 2:
@@ -364,8 +421,9 @@
             row = block_row(c, j // 2) * 2 + j % 2
             ub[pl.ds(row, 1), :] = jnp.sum(back, axis=0, keepdims=True)
 
-    over(chunks_at(HY), key_grad)
-    scatter(k_term, 0)
+    for pair in pairs(far):
+        over(pair, key_grad)
+        send_far(k_term, pair)
     for k in range(3, HY):
         scatter(v_term, k)
 
@@ -384,21 +442,20 @@
         wires.start(po.at[:, x_far, :, left], rx_half.at[0], x_peer(1)),
         wires.start(po.at[:, x_far, :, right], rx_half.at[1], x_peer(-1)),
     ]
-    for k in range(1, HY):
-        over(chunks_at(HY - k), key_grad)
-        scatter(k_term, k)
-        if k == 1:
-            over(chunks_at(0), value_grad)
-            settle(v_term)
-        if k == 2 or HY == 2:
-            arrived(o_far)
-            po[:, x_up, :, left] = (po[:, x_up, :, left].astype(F32) + rx_half[0].astype(F32)).astype(BF16)
-            po[:, x_down, :, right] = (po[:, x_down, :, right].astype(F32) + rx_half[1].astype(F32)).astype(BF16)
-            o_near = [
-                wires.start(po.at[:, x_up], rx_full.at[0], x_peer(1)),
-                wires.start(po.at[:, x_down], rx_full.at[1], x_peer(-1)),
-            ]
-    over(chunks_at(0), key_grad)
+    for pair in pairs(near):
+        over(pair, key_grad)
+        send_near(k_term, pair)
+    over([0], value_grad)
+    settle(v_term)
+    pass_on(k_term)
+    arrived(o_far)
+    po[:, x_up, :, left] = (po[:, x_up, :, left].astype(F32) + rx_half[0].astype(F32)).astype(BF16)
+    po[:, x_down, :, right] = (po[:, x_down, :, right].astype(F32) + rx_half[1].astype(F32)).astype(BF16)
+    o_near = [
+        wires.start(po.at[:, x_up], rx_full.at[0], x_peer(1)),
+        wires.start(po.at[:, x_down], rx_full.at[1], x_peer(-1)),
+    ]
+    over([0], key_grad)
 
     for h in range(G):
         cols = slice(h * HW, (h + 1) * HW)
@@ -414,7 +471,7 @@
     btile[0, G + 2:8, :] = jnp.zeros((8 - G - 2, HW), F32)
     bias_dp = wires.start(btile.at[0], b_dp, dp_peer)
 
-    settle(k_term)
+    finish_near(k_term)
 
     bias_dp.wait_recv()
     btile[1] = btile[0] + b_dp[...]
@@ -444,7 +501,7 @@
         + rz[...].astype(F32)
     ).astype(BF16)
 
-    g = total_of(k_term)
+    g = whole_of(k_term)
     kg_ref[0] = (g * cos - turn(g) * sin).astype(BF16)
 
     arrived(bias_y)
@@ -469,6 +526,13 @@
     V = pltpu.VMEM
     HY = NY // 2
     ring = [V((HY, 2, NZ, HW, HW), BF16), V((NZ - 1, HW, HW), BF16)]
+    near, far = (len(chunks) for chunks in near_and_far(NY))
+    direct = [
+        V((near, NZ, HW, HW), BF16),
+        V((far, HW, HW), BF16),
+        V((far, NZ - 1, HW, HW), BF16),
+        V((NZ - 1, HW, HW), BF16),
+    ]
     copies = 4 * (NZ - 1 + NZ * (2 * HY - 1)) + 16 + NZ + NY
     outs = pl.pallas_call(
         functools.partial(kernel, (NY, NX, G)),
@@ -498,7 +562,7 @@
             V((QN, HW), F32),
             V((NY, NZ, HW, HW), BF16),
             V((NY, NZ, HW, HW), BF16),
-            *ring,
+            *direct,
             *ring,
             V((NZL, NX, own_rows, width), BF16),
             V((2, NZL, own_rows, w_cols), BF16),

time: 90 us -> 87 us (0.967)
  Pallas kernels: 88.3 us -> 85.7 us
    pallas_call x1, Pallas kernels: 86.5 us -> 83.9 us  [layer(): pl.pallas_call(functools.partial(kernel, (NY, NX, G)), out_shape=(jax.Sha...]
where the time goes in v3:
time: 87 us; the launch traced here: 86.3 us
  Pallas kernels  85.7 us (99%)
    pallas_call x1, Pallas kernels, layer(): pl.pallas_call(functools.partial(kernel, (NY, NX, G)), out_shape=(jax.Sha...  83.9 us
    pallas_call x1, Pallas kernels, layer(): pl.pallas_call(functools.partial(finish, G), out_shape=tuple(shapes), in_...  1.78 us

profile of v3, /device:TPU:6, one launch (start us, length us, event | category | flops | bytes accessed | tf_op | source)
XLA Modules:
  0.0 86.3 jit_solution(14881221659575125209)
XLA Ops:
  0.6 83.9 %attention_layer.1 = (bf16[1,16,5120]{2,1,0:T(8,128)(2,1)}, bf16[1,128,640]{2,1,0:T(8,128)(2,1)}, bf16[1,128,128]{2,1,0:T(8,128)(2,1)}, bf16[1,128,128]{2,1,0:T(8,128)(2,1)}, f32[8,128]{1,0:T(8,128)}) custom-call(bf16[1,128,640]{2,1,0:T(8,128)(2,1)} %q_ref.1, bf16[1,128,128]{2,1,0:T(8,128)(2,1)} %k_ref.1, bf16[1,128,128]{2,1,0:T(8,128)(2,1)} %v_ref.1, ...), custom_call_target="tpu_custom_call" | custom-call | tf_op jit(solution)/shard_map/attention_layer/pallas_call | solution.py:537
  84.5 1.8 %hand_over.1 = (bf16[1,16,5120]{2,1,0:T(8,128)(2,1)}, bf16[1,128,640]{2,1,0:T(8,128)(2,1)}, bf16[1,128,128]{2,1,0:T(8,128)(2,1)}, bf16[1,128,128]{2,1,0:T(8,128)...) custom-call(bf16[1,16,5120]{2,1,0:T(8,128)(2,1)} %get-tuple-element.12.refs_0_, ...), custom_call_target="tpu_custom_call" | custom-call | tf_op jit(solution)/shard_map/hand_over/pallas_call | solution.py:595

commit v4 on v3

--- a/solution.py
+++ b/solution.py
@@ -421,12 +421,6 @@
             row = block_row(c, j // 2) * 2 + j % 2
             ub[pl.ds(row, 1), :] = jnp.sum(back, axis=0, keepdims=True)
 
-    for pair in pairs(far):
-        over(pair, key_grad)
-        send_far(k_term, pair)
-    for k in range(3, HY):
-        scatter(v_term, k)
-
     def mix(n, carry):
         half = n // n_inner
         at = pl.multiple_of(lax.rem(n, n_inner) * CHUNK, CHUNK)
@@ -442,20 +436,30 @@
         wires.start(po.at[:, x_far, :, left], rx_half.at[0], x_peer(1)),
         wires.start(po.at[:, x_far, :, right], rx_half.at[1], x_peer(-1)),
     ]
+    o_near = [
+        wires.start(po.at[:, x_up, :, right], rx_full.at[0, :, :, right], x_peer(1)),
+        wires.start(po.at[:, x_down, :, left], rx_full.at[1, :, :, left], x_peer(-1)),
+    ]
+    for pair in pairs(far):
+        over(pair, key_grad)
+        send_far(k_term, pair)
+    for k in range(3, HY):
+        scatter(v_term, k)
+
     for pair in pairs(near):
         over(pair, key_grad)
         send_near(k_term, pair)
+    arrived(o_far)
+    po[:, x_up, :, left] = (po[:, x_up, :, left].astype(F32) + rx_half[0].astype(F32)).astype(BF16)
+    po[:, x_down, :, right] = (po[:, x_down, :, right].astype(F32) + rx_half[1].astype(F32)).astype(BF16)
+    o_near += [
+        wires.start(po.at[:, x_up, :, left], rx_full.at[0, :, :, left], x_peer(1)),
+        wires.start(po.at[:, x_down, :, right], rx_full.at[1, :, :, right], x_peer(-1)),
+    ]
+    over([0], key_grad)
     over([0], value_grad)
     settle(v_term)
     pass_on(k_term)
-    arrived(o_far)
-    po[:, x_up, :, left] = (po[:, x_up, :, left].astype(F32) + rx_half[0].astype(F32)).astype(BF16)
-    po[:, x_down, :, right] = (po[:, x_down, :, right].astype(F32) + rx_half[1].astype(F32)).astype(BF16)
-    o_near = [
-        wires.start(po.at[:, x_up], rx_full.at[0], x_peer(1)),
-        wires.start(po.at[:, x_down], rx_full.at[1], x_peer(-1)),
-    ]
-    over([0], key_grad)
 
     for h in range(G):
         cols = slice(h * HW, (h + 1) * HW)

time: 87 us -> 86.4 us (level)
  no operation moved by 1% of the time
where the time goes in v4:
time: 86.4 us; the launch traced here: 86.2 us
  Pallas kernels  85.6 us (99%)
    pallas_call x1, Pallas kernels, layer(): pl.pallas_call(functools.partial(kernel, (NY, NX, G)), out_shape=(jax.Sha...  83.8 us
    pallas_call x1, Pallas kernels, layer(): pl.pallas_call(functools.partial(finish, G), out_shape=tuple(shapes), in_...  1.78 us

profile of v4, /device:TPU:6, one launch (start us, length us, event | category | flops | bytes accessed | tf_op | source)
XLA Modules:
  0.0 86.2 jit_solution(17437834810717766215)
XLA Ops:
  0.6 83.8 %attention_layer.1 = (bf16[1,16,5120]{2,1,0:T(8,128)(2,1)}, bf16[1,128,640]{2,1,0:T(8,128)(2,1)}, bf16[1,128,128]{2,1,0:T(8,128)(2,1)}, bf16[1,128,128]{2,1,0:T(8,128)(2,1)}, f32[8,128]{1,0:T(8,128)}) custom-call(bf16[1,128,640]{2,1,0:T(8,128)(2,1)} %q_ref.1, bf16[1,128,128]{2,1,0:T(8,128)(2,1)} %k_ref.1, bf16[1,128,128]{2,1,0:T(8,128)(2,1)} %v_ref.1, ...), custom_call_target="tpu_custom_call" | custom-call | tf_op jit(solution)/shard_map/attention_layer/pallas_call | solution.py:541
  84.4 1.8 %hand_over.1 = (bf16[1,16,5120]{2,1,0:T(8,128)(2,1)}, bf16[1,128,640]{2,1,0:T(8,128)(2,1)}, bf16[1,128,128]{2,1,0:T(8,128)(2,1)}, bf16[1,128,128]{2,1,0:T(8,128)...) custom-call(bf16[1,16,5120]{2,1,0:T(8,128)(2,1)} %get-tuple-element.12.refs_0_, ...), custom_call_target="tpu_custom_call" | custom-call | tf_op jit(solution)/shard_map/hand_over/pallas_call | solution.py:599

commit v5 on v4

--- a/solution.py
+++ b/solution.py
@@ -84,7 +84,7 @@
     q_ref, k_ref, v_ref, qb_ref, kbias_ref, vbias_ref, freq_ref, bp_ref, doc_ref, w_hbm, og_hbm,
     out_ref, qg_ref, kg_ref, vg_ref, bias_ref,
     qn, qt, kb, vb, sb, eb, wb, og, dot_t, dot_n, o_rows, acc_o, acc_q, acc_g,
-    pk, pv, rk, rk_f, rk_m, rk_z, rv, rv_z,
+    pk, pv, rk, rk_f, rk_m, rk_z, rv, rv_f, rv_m, rv_z,
     po, rx_half, rx_full, rz, zs, mb, lb, ub, bpv, vs, btile, b_dp, b_z, b_y,
     local_sem, send_sem, recv_sem,
 ):
@@ -385,21 +385,18 @@
             g = g + term.landing[r].astype(F32)
         return g
 
-    v_term, k_term = Term(pv, rv, rv_z), Direct(pk, rk, rk_f, rk_m, rk_z)
-
-    over(chunks_at(HY), value_grad)
-    scatter(v_term, 0)
-    forward(vb, v_in, HY - 1, order)
-    over(chunks_at(HY - 1), value_grad)
-    scatter(v_term, 1)
-    if HY > 2:
-        over(chunks_at(HY - 2), value_grad)
+    v_term, k_term = Direct(pv, rv, rv_f, rv_m, rv_z), Direct(pk, rk, rk_f, rk_m, rk_z)
+
+    for n, pair in enumerate(pairs(far)):
+        over(pair, value_grad)
+        send_far(v_term, pair)
+        if n == 0:
+            forward(vb, v_in, HY - 1, order)
+    for pair in pairs(near):
+        over(pair, value_grad)
+        send_near(v_term, pair)
     for k in range(HY):
         over(chunks_at(k), attend)
-    if HY > 2:
-        scatter(v_term, 2)
-    for k in range(1, HY - 2):
-        over(chunks_at(k), value_grad)
     for r in range(NZ):
         arrived(v_in[HY, r])
     over(chunks_at(HY), attend)
@@ -443,8 +440,7 @@
     for pair in pairs(far):
         over(pair, key_grad)
         send_far(k_term, pair)
-    for k in range(3, HY):
-        scatter(v_term, k)
+    pass_on(v_term)
 
     for pair in pairs(near):
         over(pair, key_grad)
@@ -458,7 +454,7 @@
     ]
     over([0], key_grad)
     over([0], value_grad)
-    settle(v_term)
+    finish_near(v_term)
     pass_on(k_term)
 
     for h in range(G):
@@ -495,7 +491,7 @@
     btile[2] = total
     bias_y = [wires.start(btile.at[2], b_y.at[d - 1], y_peer(d)) for d in range(1, NY)]
 
-    vg_ref[0] = total_of(v_term).astype(BF16)
+    vg_ref[0] = whole_of(v_term).astype(BF16)
 
     o_z.wait_recv()
     out_ref[0] = (
@@ -567,7 +563,7 @@
             V((NY, NZ, HW, HW), BF16),
             V((NY, NZ, HW, HW), BF16),
             *direct,
-            *ring,
+            *direct,
             V((NZL, NX, own_rows, width), BF16),
             V((2, NZL, own_rows, w_cols), BF16),
             V((2, NZL, own_rows, width), BF16),

time: 86.4 us -> 84.4 us (0.977)
  the two profiles are of different devices: /device:TPU:6 before, /device:TPU:2 now
where the time goes in v5:
time: 84.4 us; the launch traced here: 84.2 us
  Pallas kernels  83.6 us (99%)
    pallas_call x1, Pallas kernels, layer(): pl.pallas_call(functools.partial(kernel, (NY, NX, G)), out_shape=(jax.Sha...  81.8 us
    pallas_call x1, Pallas kernels, layer(): pl.pallas_call(functools.partial(finish, G), out_shape=tuple(shapes), in_...  1.78 us

profile of v5, /device:TPU:2, one launch (start us, length us, event | category | flops | bytes accessed | tf_op | source)
XLA Modules:
  0.0 84.2 jit_solution(12767146430897996026)
XLA Ops:
  0.6 81.8 %attention_layer.1 = (bf16[1,16,5120]{2,1,0:T(8,128)(2,1)}, bf16[1,128,640]{2,1,0:T(8,128)(2,1)}, bf16[1,128,128]{2,1,0:T(8,128)(2,1)}, bf16[1,128,128]{2,1,0:T(8,128)(2,1)}, f32[8,128]{1,0:T(8,128)}) custom-call(bf16[1,128,640]{2,1,0:T(8,128)(2,1)} %q_ref.1, bf16[1,128,128]{2,1,0:T(8,128)(2,1)} %k_ref.1, bf16[1,128,128]{2,1,0:T(8,128)(2,1)} %v_ref.1, ...), custom_call_target="tpu_custom_call" | custom-call | tf_op jit(solution)/shard_map/attention_layer/pallas_call | solution.py:537
  82.4 1.8 %hand_over.1 = (bf16[1,16,5120]{2,1,0:T(8,128)(2,1)}, bf16[1,128,640]{2,1,0:T(8,128)(2,1)}, bf16[1,128,128]{2,1,0:T(8,128)(2,1)}, bf16[1,128,128]{2,1,0:T(8,128)...) custom-call(bf16[1,16,5120]{2,1,0:T(8,128)(2,1)} %get-tuple-element.12.refs_0_, ...), custom_call_target="tpu_custom_call" | custom-call | tf_op jit(solution)/shard_map/hand_over/pallas_call | solution.py:595
